TPU v7x, 512 devices: a whole 4x8x8 slice. The times are simulated.
512 devices in a mesh: group: 8 (over z), tensor: 8 (over x, core), ctx: 8 (over y).
Axes of the slice: x: 4, y: 8, z: 8, core: 2. Of those that a mesh axis runs over, the one named last changes fastest.
Arguments:
- cache_keys: bfloat16 [32, 4096, 1024], P('group', 'ctx', 'tensor'), may hold values from -6 to 6
- cache_values: bfloat16 [32, 4096, 1024], P('group', 'ctx', 'tensor'), may hold values from -6 to 6
- sink_keys: bfloat16 [32, 4, 1024], P('group', None, 'tensor'), may hold values from -21 to 21
- sink_values: bfloat16 [32, 4, 1024], P('group', None, 'tensor'), may hold values from -6 to 6
- turn_queries: bfloat16 [32, 384, 12288], P('group', 'ctx', 'tensor'), may hold values from -160 to 160
- turn_keys: bfloat16 [32, 384, 1024], P('group', 'ctx', 'tensor'), may hold values from -4.5 to 4.5
- turn_values: bfloat16 [32, 384, 1024], P('group', 'ctx', 'tensor'), may hold values from -6 to 6
- decode_queries: bfloat16 [32, 2, 12288], P('group', None, 'tensor'), may hold values from -160 to 160
- decode_keys: bfloat16 [32, 2, 1024], P('group', None, 'tensor'), may hold values from -6 to 6
- decode_values: bfloat16 [32, 2, 1024], P('group', None, 'tensor'), may hold values from -6 to 6
- turn_lengths: int32 [32], P('group'), may hold values from 16 to 384, as said below
- history: int32 [32], P('group'), may hold values from 516 to 8191
- targets: int32 [32, 1], P('group'), may hold values from 0 to 7; in each aligned block of 4 rows (0 to 3, 4 to 7, ...) no two rows name the same one
Outputs:
- turn_out: bfloat16 [64, 384, 12288], P(('group', 'ctx'), None, 'tensor')
- decode_out: bfloat16 [64, 2, 12288], P(('group', 'ctx'), None, 'tensor')
- moved_keys: bfloat16 [64, 4096, 1024], P(('group', 'ctx'), None, 'tensor')
- moved_values: bfloat16 [64, 4096, 1024], P(('group', 'ctx'), None, 'tensor')
Inputs may be any that keep to these rules, and one draw needn't show every extreme that they name: `turn_lengths`: some session has exactly 384 tokens and some exactly 16. `targets`: the 4 sessions of one home group (aligned blocks of 4 sessions) go to different groups.
All inputs are finite; a program needn't handle non-finite values.
Results may differ from a plain program's by a relative error of at most 0.0055.
Values may be sent and summed in bfloat16 or wider, within the bound.
A program may use at most 64 MiB of HBM per device.

v0:
```python
import math

import jax
import jax.numpy as jnp
from jax import lax
from jax.sharding import PartitionSpec as P

HEADS = 96
KV_HEADS = 8
HEAD_DIM = 128
WINDOW = 4096
SINKS = 4


NEG = -1e30


def merged_2(part, axis, combine):
    gathered = jax.tree.map(lambda a: lax.all_gather(a, axis), part)

    def take(source):
        return jax.tree.map(lambda a: lax.dynamic_index_in_dim(a, source, 0, False), gathered)

    return lax.fori_loop(
        1, lax.axis_size(axis), lambda source, state: combine(state, take(source)), take(0)
    )


def empty_state(sessions, key_heads, group_size, count, head_dim):
    shape = (sessions, key_heads, group_size, count, 1)
    return (
        jnp.full(shape, NEG, jnp.float32),
        jnp.zeros(shape, jnp.float32),
        jnp.zeros((sessions, key_heads, group_size, count, head_dim), jnp.float32),
    )


def masked_update(state, queries, key_block, value_block, visible):
    peak, weight_sum, weighted = state
    scale = 1.0 / math.sqrt(key_block.shape[-1])
    scores = (
        jnp.einsum("sqkgd,snkd->skgqn", queries, key_block, preferred_element_type=jnp.float32)
        * scale
    )
    allowed = visible[:, None, None, :, :]
    scores = jnp.where(allowed, scores, NEG)
    new_peak = jnp.maximum(peak, jnp.max(scores, axis=-1, keepdims=True))
    weights = jnp.where(allowed, jnp.exp(scores - new_peak), 0.0)
    factor = jnp.exp(peak - new_peak)
    weight_sum = weight_sum * factor + jnp.sum(weights, axis=-1, keepdims=True)
    weighted = weighted * factor + jnp.einsum(
        "skgqn,snkd->skgqd",
        weights.astype(jnp.bfloat16),
        value_block,
        preferred_element_type=jnp.float32,
    )
    return (new_peak, weight_sum, weighted)


def combine(first, second):
    peak = jnp.maximum(first[0], second[0])
    left = jnp.exp(first[0] - peak)
    right = jnp.exp(second[0] - peak)
    return (peak, first[1] * left + second[1] * right, first[2] * left + second[2] * right)


def heads_last(state):
    result = state[2] / state[1]
    sessions, key_heads, group_size, count, head_dim = result.shape
    return result.transpose(0, 3, 1, 2, 4).reshape(
        sessions, count, key_heads * group_size * head_dim
    )


def shards(
    cache_keys,
    cache_values,
    sink_keys,
    sink_values,
    turn_queries,
    turn_keys,
    turn_values,
    decode_queries,
    decode_keys,
    decode_values,
    turn_lengths,
    history,
    targets,
):
    sessions, win_rows, key_width = cache_keys.shape
    turn_rows = turn_queries.shape[1]
    decode_rows = decode_queries.shape[1]
    head_dim = HEAD_DIM
    key_heads = key_width // head_dim
    group_size = HEADS // KV_HEADS
    context_index = lax.axis_index("ctx")
    context_count = lax.axis_size("ctx")
    group_count = lax.axis_size("group")
    block_rows = win_rows + turn_rows
    turn_q = turn_queries.reshape(sessions, turn_rows, key_heads, group_size, head_dim)
    decode_q = decode_queries.reshape(sessions, decode_rows, key_heads, group_size, head_dim)
    query_ids = context_index * turn_rows + jnp.arange(turn_rows, dtype=jnp.int32)
    step_ids = jnp.arange(decode_rows, dtype=jnp.int32)
    front_rows = SINKS + decode_rows
    front_keys = jnp.concatenate([sink_keys, decode_keys], axis=1).reshape(
        sessions, front_rows, key_heads, head_dim
    )
    front_values = jnp.concatenate([sink_values, decode_values], axis=1).reshape(
        sessions, front_rows, key_heads, head_dim
    )
    front_ids = jnp.arange(front_rows, dtype=jnp.int32)
    is_sink = front_ids < SINKS
    turn_front = jnp.broadcast_to(is_sink[None, None, :], (sessions, turn_rows, front_rows))
    decode_front = jnp.broadcast_to(
        (is_sink[None, :] | (front_ids[None, :] - SINKS <= step_ids[:, None]))[None],
        (sessions, decode_rows, front_rows),
    )
    turn_start = masked_update(
        empty_state(sessions, key_heads, group_size, turn_rows, head_dim),
        turn_q,
        front_keys,
        front_values,
        turn_front,
    )
    decode_start = masked_update(
        empty_state(sessions, key_heads, group_size, decode_rows, head_dim),
        decode_q,
        front_keys,
        front_values,
        decode_front,
    )
    local_keys = jnp.concatenate([cache_keys, turn_keys], axis=1)
    local_values = jnp.concatenate([cache_values, turn_values], axis=1)

    def block_masks(device):
        column_ids = jnp.arange(block_rows, dtype=jnp.int32)
        in_window = column_ids < win_rows
        window_ids = device * win_rows + column_ids
        turn_ids = device * turn_rows + column_ids - win_rows
        history_ok = history[:, None] - WINDOW + window_ids[None, :] >= SINKS
        turn_mask = jnp.where(
            in_window[None, None, :],
            history_ok[:, None, :] & (window_ids[None, None, :] > query_ids[None, :, None]),
            turn_ids[None, None, :] <= query_ids[None, :, None],
        )
        limit_rows = turn_lengths[:, None] + step_ids[None, :]
        decode_mask = jnp.where(
            in_window[None, None, :],
            history_ok[:, None, :] & (window_ids[None, None, :] > limit_rows[:, :, None]),
            turn_ids[None, None, :] < turn_lengths[:, None, None],
        )
        return (turn_mask, decode_mask)

    def block_at(part_rows, number):
        return lax.dynamic_slice_in_dim(part_rows, number * block_rows, block_rows, 1).reshape(
            sessions, block_rows, key_heads, head_dim
        )

    chooser = (targets[:, 0][None, :] == jnp.arange(group_count, dtype=jnp.int32)[:, None]).astype(
        jnp.bfloat16
    )

    def to_targets(values):
        return jnp.einsum(
            "ts,s...->t...", chooser, values, preferred_element_type=jnp.float32
        ).astype(jnp.bfloat16)

    part_keys = lax.all_gather(local_keys, "ctx", axis=1, tiled=True)
    part_values = lax.all_gather(local_values, "ctx", axis=1, tiled=True)

    def advance(number, inner):
        turn_mask, decode_mask = block_masks(number)
        return masked_update(
            inner, turn_q, block_at(part_keys, number), block_at(part_values, number), turn_mask
        )

    turn_state = lax.fori_loop(0, part_keys.shape[1] // block_rows, advance, turn_start)
    own_turn, own_decode = block_masks(context_index)
    own_state = masked_update(
        empty_state(sessions, key_heads, group_size, decode_rows, head_dim),
        decode_q,
        local_keys.reshape(sessions, block_rows, key_heads, head_dim),
        local_values.reshape(sessions, block_rows, key_heads, head_dim),
        own_decode,
    )
    merged = merged_2(own_state, "ctx", combine)
    decode_state = combine(merged, decode_start)
    live = query_ids[None, :, None] < turn_lengths[:, None, None]
    turn_home = jnp.where(live, heads_last(turn_state), 0.0).astype(jnp.bfloat16)
    decode_home = heads_last(decode_state).astype(jnp.bfloat16)
    moved_turn, moved_keys, moved_values = (
        lax.all_to_all(
            lax.all_to_all(to_targets(turn_home), "group", split_axis=0, concat_axis=0, tiled=True),
            "ctx",
            split_axis=0,
            concat_axis=1,
            tiled=True,
        ),
        lax.all_to_all(
            lax.all_to_all(
                to_targets(cache_keys), "group", split_axis=0, concat_axis=0, tiled=True
            ),
            "ctx",
            split_axis=0,
            concat_axis=1,
            tiled=True,
        ),
        lax.all_to_all(
            lax.all_to_all(
                to_targets(cache_values), "group", split_axis=0, concat_axis=0, tiled=True
            ),
            "ctx",
            split_axis=0,
            concat_axis=1,
            tiled=True,
        ),
    )
    arrivals = lax.all_to_all(
        to_targets(decode_home), "group", split_axis=0, concat_axis=0, tiled=True
    )
    per_device = group_count // context_count
    moved_decode = lax.dynamic_slice_in_dim(arrivals, context_index * per_device, per_device, 0)
    return (moved_turn, moved_decode, moved_keys, moved_values)


def solution(mesh):
    return jax.shard_map(
        shards,
        mesh=mesh,
        in_specs=(
            P("group", "ctx", "tensor"),
            P("group", "ctx", "tensor"),
            P("group", None, "tensor"),
            P("group", None, "tensor"),
            P("group", "ctx", "tensor"),
            P("group", "ctx", "tensor"),
            P("group", "ctx", "tensor"),
            P("group", None, "tensor"),
            P("group", None, "tensor"),
            P("group", None, "tensor"),
            P("group"),
            P("group"),
            P("group", None),
        ),
        out_specs=(
            P(("group", "ctx"), None, "tensor"),
            P(("group", "ctx"), None, "tensor"),
            P(("group", "ctx"), None, "tensor"),
            P(("group", "ctx"), None, "tensor"),
        ),
        check_vma=False,
    )
```

profile of v0, /device:TPU:2, one launch (start us, length us, event | category | flops | bytes accessed | tf_op | source)
XLA Modules:
  0.0 339.3 jit_solution(11836309734732586722)
XLA Ops:
  17.3 26.1 %all-gather = f32[32,12,2]{1,2,0:T(2,128)S(1)} all-gather(f32[4,12,2]{1,2,0:T(2,128)S(1)} %broadcast_maximum_fusion.2), channel_id=2, replica_groups=mesh['group'=8,'tensor'=8,'ctx'=8] {'ctx'}, dimensions={0}, use_global_device_ids=true | all-gather | bytes 3456 | tf_op jit(solution)/shard_map/all_gather | solution.py:19
  45.0 26.1 %all-gather.1 = f32[32,12,2,128]{3,2,1,0:T(2,128)S(1)} all-gather(f32[4,12,2,128]{3,2,1,0:T(2,128)S(1)} %copy.67), channel_id=3, replica_groups=mesh['group'=8,'tensor'=8,'ctx'=8] {'ctx'}, dimensions={0}, use_global_device_ids=true | all-gather | bytes 442368 | tf_op jit(solution)/shard_map/all_gather | solution.py:19
  71.1 24.5 %all_gather.23 = f32[8,4,1,12,2,1]{3,1,5,4,2,0:T(4,128)S(1)} all-gather(f32[1,4,1,12,2,1]{3,1,5,4,2,0:T(4,128)S(1)} %bitcast.268), channel_id=1, replica_groups=mesh['group'=8,'tensor'=8,'ctx'=8] {'ctx'}, dimensions={0}, use_global_device_ids=true | all-gather | bytes 3456 | tf_op jit(solution)/shard_map/all_gather | solution.py:19
  95.6 4.5 %while.39 = (s32[]{:T(128)}, f32[4,1,12,2,1]{2,0,4,3,1:T(4,128)S(1)}, f32[4,1,12,2,1]{2,0,4,3,1:T(4,128)S(1)}, f32[4,1,12,2,128]{4,3,2,1,0:T(2,128)S(1)}, f32[8,...) while((s32[]{:T(128)}, ...), condition=%wide.region_9.10_spmd, body=%wide.region_8.9_spmd.sunk | while | flops 37541 | bytes 155675 | solution.py:24
  101.8 10.5 %all-to-all-start.2 = ((bf16[8,2,1536]{2,1,0:T(2,128)(2,1)}), bf16[8,2,1536]{2,1,0:T(2,128)(2,1)S(1)}, u32[]{:S(2)}, u32[]{:S(2)}) async-start(bf16[8,2,1536]{2,1,0:T(2,128)(2,1)} %copy.79), calls=%async_computation.2 | async-start | bytes 98304 | tf_op jit(solution)/shard_map/all_to_all | solution.py:218
  114.2 7.1 %all-to-all-done.2 = bf16[8,2,1536]{2,1,0:T(2,128)(2,1)S(1)} async-done(((bf16[8,2,1536]{2,1,0:T(2,128)(2,1)}), bf16[8,2,1536]{2,1,0:T(2,128)(2,1)S(1)}, u32[]{:S(2)}, u32[]{:S(2)}) %all-to-all-start.2) | async-done | bytes 49184 | tf_op jit(solution)/shard_map/all_to_all | solution.py:218
  121.3 4.6 %all-to-all-start.3 = ((bf16[8,512,128]{2,1,0:T(8,128)(2,1)}), bf16[8,512,128]{2,1,0:T(8,128)(2,1)}, u32[]{:S(2)}, u32[]{:S(2)}) async-start(bf16[8,512,128]{2,1,0:T(8,128)(2,1)} %copy.81), calls=%async_computation.3 | async-start | bytes 2097152 | tf_op jit(solution)/shard_map/all_to_all | solution.py:200
  126.6 25.5 %all-to-all-done.3 = bf16[8,512,128]{2,1,0:T(8,128)(2,1)} async-done(((bf16[8,512,128]{2,1,0:T(8,128)(2,1)}), bf16[8,512,128]{2,1,0:T(8,128)(2,1)}, u32[]{:S(2)}, u32[]{:S(2)}) %all-to-all-start.3) | async-done | bytes 1048608 | tf_op jit(solution)/shard_map/all_to_all | solution.py:200
  152.1 22.4 %all_to_all.56 = bf16[8,512,128]{2,1,0:T(8,128)(2,1)} all-to-all(bf16[8,512,128]{2,1,0:T(8,128)(2,1)S(1)} %copy.83), channel_id=1, replica_groups=mesh['group'=8,'tensor'=8,'ctx'=8] {'group'}, dimensions={0} | all-to-all | bytes 2097152 | tf_op jit(solution)/shard_map/all_to_all | solution.py:209
  174.5 5.7 %all-to-all-start.4 = ((bf16[8,512,128]{2,1,0:T(8,128)(2,1)}), bf16[8,512,128]{2,1,0:T(8,128)(2,1)S(1)}, u32[]{:S(2)}, u32[]{:S(2)}) async-start(bf16[8,512,128]{2,1,0:T(8,128)(2,1)} %all-to-all-done.3), calls=%async_computation.4 | async-start | bytes 2097152 | tf_op jit(solution)/shard_map/all_to_all | solution.py:199
  182.3 27.9 %all-to-all-done.4 = bf16[8,512,128]{2,1,0:T(8,128)(2,1)S(1)} async-done(((bf16[8,512,128]{2,1,0:T(8,128)(2,1)}), bf16[8,512,128]{2,1,0:T(8,128)(2,1)S(1)}, u32[]{:S(2)}, u32[]{:S(2)}) %all-to-all-start.4) | async-done | bytes 1048608 | tf_op jit(solution)/shard_map/all_to_all | solution.py:199
  210.2 4.4 %all-to-all-start.6 = ((bf16[8,512,128]{2,1,0:T(8,128)(2,1)}), bf16[8,512,128]{2,1,0:T(8,128)(2,1)}, u32[]{:S(2)}, u32[]{:S(2)}) async-start(bf16[8,512,128]{2,1,0:T(8,128)(2,1)} %all_to_all.56), calls=%async_computation.6 | async-start | bytes 2097152 | tf_op jit(solution)/shard_map/all_to_all | solution.py:208
  214.7 60.6 %while.40 = (s32[]{:T(128)}, f32[4,1,12,48,1]{3,2,0,4,1:T(8,128)S(1)}, f32[4,1,12,48,1]{3,2,0,4,1:T(8,128)S(1)}, f32[4,1,12,48,128]{4,3,2,0,1:T(8,128)S(1)}, s32...) while((s32[]{:T(128)}, ...), condition=%wide.region_5.6_spmd.clone, body=%wide.region_2.0_spmd.clone.sunk | while | flops 678248320 | bytes 20281400 | solution.py:177
  217.4 2.9 fusion.122
  225.0 2.9 fusion.122
  232.5 2.9 fusion.122
  240.1 2.9 fusion.122
  247.7 2.9 fusion.122
  255.3 2.9 fusion.122
  262.8 2.9 fusion.122
  270.4 2.9 fusion.122
  277.6 23.4 %all_to_all.57 = bf16[8,48,1536]{2,1,0:T(8,128)(2,1)} all-to-all(bf16[8,48,1536]{2,1,0:T(8,128)(2,1)S(1)} %copy.64), channel_id=1, replica_groups=mesh['group'=8,'tensor'=8,'ctx'=8] {'group'}, dimensions={0} | all-to-all | bytes 2359296 | tf_op jit(solution)/shard_map/all_to_all | solution.py:193
  301.0 6.9 %all-to-all-start.1 = ((bf16[8,48,1536]{2,1,0:T(8,128)(2,1)}), bf16[8,48,1536]{2,1,0:T(8,128)(2,1)S(1)}, u32[]{:S(2)}, u32[]{:S(2)}) async-start(bf16[8,48,1536]{2,1,0:T(8,128)(2,1)} %all_to_all.57), calls=%async_computation.1 | async-start | bytes 2359296 | tf_op jit(solution)/shard_map/all_to_all | solution.py:192
  308.4 19.8 %all-to-all-done.1 = bf16[8,48,1536]{2,1,0:T(8,128)(2,1)S(1)} async-done(((bf16[8,48,1536]{2,1,0:T(8,128)(2,1)}), bf16[8,48,1536]{2,1,0:T(8,128)(2,1)S(1)}, u32[]{:S(2)}, u32[]{:S(2)}) %all-to-all-start.1) | async-done | bytes 1179680 | tf_op jit(solution)/shard_map/all_to_all | solution.py:192
  (236 shorter events, 65.5 us)
Async XLA Ops:
  7.2 93.0 %copy-start.6 = (bf16[4,4,128]{2,1,0:T(4,128)(2,1)S(1)}, bf16[4,4,128]{2,1,0:T(4,128)(2,1)}, u32[]{:S(2)}) copy-start(bf16[4,4,128]{2,1,0:T(4,128)(2,1)} %param.19) | copy-start | bytes 12292
  7.2 93.0 %copy-start.8 = (bf16[4,2,128]{2,1,0:T(2,128)(2,1)S(1)}, bf16[4,2,128]{2,1,0:T(2,128)(2,1)}, u32[]{:S(2)}) copy-start(bf16[4,2,128]{2,1,0:T(2,128)(2,1)} %param.25) | copy-start | bytes 6148
  7.2 93.4 %copy-start.7 = (bf16[4,4,128]{2,1,0:T(4,128)(2,1)S(1)}, bf16[4,4,128]{2,1,0:T(4,128)(2,1)}, u32[]{:S(2)}) copy-start(bf16[4,4,128]{2,1,0:T(4,128)(2,1)} %param.20) | copy-start | bytes 12292
  7.2 93.4 %copy-start.9 = (bf16[4,2,128]{2,1,0:T(2,128)(2,1)S(1)}, bf16[4,2,128]{2,1,0:T(2,128)(2,1)}, u32[]{:S(2)}) copy-start(bf16[4,2,128]{2,1,0:T(2,128)(2,1)} %param.26) | copy-start | bytes 6148
  7.2 207.5 %all-gather.5.cloned.1.call-start = ((), (), s32[]{:S(2)}) async-start(), calls=%async_computation.7 | async-start | bytes 5160960 | tf_op jit(solution)/shard_map/all_gather | solution.py:168
  8.3 92.5 %copy-start.5 = (s32[4,1]{0,1:T(1,128)S(1)}, s32[4,1]{0,1:T(1,128)}, u32[]{:S(2)}) copy-start(s32[4,1]{0,1:T(1,128)} %param.29) | copy-start | bytes 52
  8.3 104.0 %copy-start.3 = (bf16[4,512,128]{2,1,0:T(8,128)(2,1)S(1)}, bf16[4,512,128]{2,1,0:T(8,128)(2,1)}, u32[]{:S(2)}) copy-start(bf16[4,512,128]{2,1,0:T(8,128)(2,1)} %param.17) | copy-start | bytes 1572868
  9.2 0.8 copy-start
  10.1 204.6 %all-gather.7.cloned.1.call-start = ((), (), s32[]{:S(2)}) async-start(), calls=%async_computation.8 | async-start | bytes 5160960 | tf_op jit(solution)/shard_map/all_gather | solution.py:169
  12.0 0.8 copy-start.2
  95.6 30.2 %copy-start.4 = (bf16[4,512,128]{2,1,0:T(8,128)(2,1)S(1)}, bf16[4,512,128]{2,1,0:T(8,128)(2,1)}, u32[]{:S(2)}) copy-start(bf16[4,512,128]{2,1,0:T(8,128)(2,1)} %param.18) | copy-start | bytes 1572868
  101.8 19.4 %all-to-all-start.2 = ((bf16[8,2,1536]{2,1,0:T(2,128)(2,1)}), bf16[8,2,1536]{2,1,0:T(2,128)(2,1)S(1)}, u32[]{:S(2)}, u32[]{:S(2)}) async-start(bf16[8,2,1536]{2,1,0:T(2,128)(2,1)} %copy.79), calls=%async_computation.2 | async-start | bytes 98304 | tf_op jit(solution)/shard_map/all_to_all | solution.py:218
  114.1 66.0 %copy-start.1 = (bf16[4,48,1536]{2,1,0:T(8,128)(2,1)S(1)}, bf16[4,48,1536]{2,1,0:T(8,128)(2,1)}, u32[]{:S(2)}) copy-start(bf16[4,48,1536]{2,1,0:T(8,128)(2,1)} %param.21) | copy-start | bytes 1769476
  121.3 30.9 %all-to-all-start.3 = ((bf16[8,512,128]{2,1,0:T(8,128)(2,1)}), bf16[8,512,128]{2,1,0:T(8,128)(2,1)}, u32[]{:S(2)}, u32[]{:S(2)}) async-start(bf16[8,512,128]{2,1,0:T(8,128)(2,1)} %copy.81), calls=%async_computation.3 | async-start | bytes 2097152 | tf_op jit(solution)/shard_map/all_to_all | solution.py:200
  126.6 55.6 %copy-start.10 = (s32[4]{0:T(128)S(1)}, s32[4]{0:T(128)}, u32[]{:S(2)}) copy-start(s32[4]{0:T(128)} %param.27) | copy-start | bytes 52
  174.5 40.2 %copy-start.11 = (s32[4]{0:T(128)S(1)}, s32[4]{0:T(128)}, u32[]{:S(2)}) copy-start(s32[4]{0:T(128)} %param.28) | copy-start | bytes 52
  174.5 35.7 %all-to-all-start.4 = ((bf16[8,512,128]{2,1,0:T(8,128)(2,1)}), bf16[8,512,128]{2,1,0:T(8,128)(2,1)S(1)}, u32[]{:S(2)}, u32[]{:S(2)}) async-start(bf16[8,512,128]{2,1,0:T(8,128)(2,1)} %all-to-all-done.3), calls=%async_computation.4 | async-start | bytes 2097152 | tf_op jit(solution)/shard_map/all_to_all | solution.py:199
  210.2 67.3 %all-to-all-start.6 = ((bf16[8,512,128]{2,1,0:T(8,128)(2,1)}), bf16[8,512,128]{2,1,0:T(8,128)(2,1)}, u32[]{:S(2)}, u32[]{:S(2)}) async-start(bf16[8,512,128]{2,1,0:T(8,128)(2,1)} %all_to_all.56), calls=%async_computation.6 | async-start | bytes 2097152 | tf_op jit(solution)/shard_map/all_to_all | solution.py:208
  301.0 27.2 %all-to-all-start.1 = ((bf16[8,48,1536]{2,1,0:T(8,128)(2,1)}), bf16[8,48,1536]{2,1,0:T(8,128)(2,1)S(1)}, u32[]{:S(2)}, u32[]{:S(2)}) async-start(bf16[8,48,1536]{2,1,0:T(8,128)(2,1)} %all_to_all.57), calls=%async_computation.1 | async-start | bytes 2359296 | tf_op jit(solution)/shard_map/all_to_all | solution.py:192
Sparse Core Ops, SparseCore 0:
  10.7 69.3 all-gather.4
  82.8 59.8 all-gather.6
where the time goes:
time: 341 us; the launch traced here: 339 us
  blocking collectives  122 us (36%)
  waiting for transfers between devices  80.3 us (24%)
  matrix products  48.5 us (14%)
  starting transfers between devices  32.2 us (9%)
  other arithmetic  24 us (7%)
  local copies, waits for them, and re-layouts  16.3 us (5%)
  between operations  14.5 us (4%)
    all_gather x3, blocking collectives, merged_2(): gathered = jax.tree.map(lambda a: lax.all_gather(a, axis), part)  76.6 us
    all_to_all x1, waiting for transfers between devices, shards(): lax.all_to_all(lax.all_to_all(to_targets(cache_keys), 'group', split_axis...  27.9 us
    dot_general x11, matrix products, masked_update(): jnp.einsum('skgqn,snkd->skgqd', weights.astype(jnp.bfloat16), value_block...  25.6 us
    all_to_all x1, waiting for transfers between devices, shards(): lax.all_to_all(to_targets(cache_keys), 'group', split_axis=0, concat_axis...  25.5 us
    all_to_all x1, blocking collectives, shards(): lax.all_to_all(to_targets(turn_home), 'group', split_axis=0, concat_axis=...  23.4 us
    all_to_all x1, blocking collectives, shards(): lax.all_to_all(to_targets(cache_values), 'group', split_axis=0, concat_ax...  22.4 us
    dot_general x11, matrix products, masked_update(): jnp.einsum('sqkgd,snkd->skgqn', queries, key_block, preferred_element_typ...  20.6 us
    all_to_all x1, waiting for transfers between devices, shards(): lax.all_to_all(lax.all_to_all(to_targets(turn_home), 'group', split_axis=...  19.8 us
  transfers between devices with their start and end apart: 7, of which 4 were waited for; matrix products, arithmetic and copies ran while one was open for 24% of the time, Pallas kernels for 0%

commit v1 on v0

v1 whole, which is shorter than its diff:
```python
import functools
import math

import jax
import jax.numpy as jnp
from jax import lax
from jax.experimental import pallas as pl
from jax.experimental.pallas import tpu as pltpu
from jax.sharding import PartitionSpec as P

HEAD_DIM = 128
SINKS = 4
NEG = -1e30
MESH = pl.DeviceIdType.MESH
PAD = 16
QUERY_STAGES = 6
AHEAD = 3


def kernel(
    ring,
    stages,
    lengths,
    history,
    targets,
    cache_k,
    cache_v,
    sink_k,
    sink_v,
    turn_q,
    turn_k,
    turn_v,
    decode_q,
    decode_k,
    decode_v,
    turn_out,
    decode_out,
    keys_out,
    values_out,
    send,
    stage,
    final,
    small_send,
    small_meta,
    small,
    meta,
    peak,
    total,
    bias,
    z_send,
    z_recv,
    y_send,
    y_recv,
    own_sem,
    small_send_sem,
    small_recv_sem,
    small_own_sem,
    out_sem,
):
    z = lax.axis_index("group")
    tensor = lax.axis_index("tensor")
    y = lax.axis_index("ctx")
    sessions, window_rows, _ = cache_k.shape
    turn_rows = turn_k.shape[1]
    heads = turn_q.shape[2] // HEAD_DIM
    steps = decode_q.shape[1]
    window = window_rows * ring
    turn = turn_rows * ring
    query_rows = turn + PAD
    head_rows = (heads + 2) * turn_rows
    query_size = head_rows // QUERY_STAGES
    chunk = window_rows // stages
    key_size = 2 * chunk
    width = ring * chunk
    scale = math.log2(math.e) / math.sqrt(HEAD_DIM)

    def around(place, step):
        return lax.rem(place + step + ring, ring)

    barrier = pltpu.get_barrier_semaphore()
    for step in range(1, ring):
        pl.semaphore_signal(
            barrier, inc=1, device_id=(around(z, step), tensor, y), device_id_type=MESH
        )
        pl.semaphore_signal(
            barrier, inc=1, device_id=(z, tensor, around(y, step)), device_id_type=MESH
        )

    def chosen(target):
        named = jnp.int32(0)
        active = jnp.int32(0)
        for s in range(sessions):
            hit = (targets[s] == target).astype(jnp.int32)
            named = jnp.maximum(named, s * hit)
            active = jnp.maximum(active, hit)
        return named, active

    def put(step, place, size, value):
        @pl.when(step == 0)
        def _():
            stage[0, pl.ds(place, size), :] = value

        @pl.when(step != 0)
        def _():
            send[step, pl.ds(place, size), :] = value

    def prepare_queries(step, carry):
        named, active = chosen(around(z, step))
        live = active.astype(jnp.float32).astype(jnp.bfloat16)
        for head in range(heads):
            columns = slice(head * HEAD_DIM, (head + 1) * HEAD_DIM)
            put(step, head * turn_rows, turn_rows, turn_q[named, :, columns] * live)
        put(step, heads * turn_rows, turn_rows, turn_k[named] * live)
        put(step, (heads + 1) * turn_rows, turn_rows, turn_v[named] * live)
        return carry

    def prepare_window(step, carry):
        named, active = chosen(around(z, step))
        live = active.astype(jnp.float32).astype(jnp.bfloat16)
        for number in range(stages):
            rows = slice(number * chunk, (number + 1) * chunk)
            place = head_rows + number * key_size
            put(step, place, chunk, cache_k[named, rows, :] * live)
            put(step, place + chunk, chunk, cache_v[named, rows, :] * live)
        return carry

    def prepare_small(step, carry):
        named, active = chosen(around(z, step))
        live = active.astype(jnp.float32).astype(jnp.bfloat16)
        small_send[step] = jnp.zeros(small_send.shape[1:], jnp.bfloat16)
        small_send[step, 0:SINKS, :] = sink_k[named] * live
        small_send[step, PAD : PAD + steps, :] = decode_k[named] * live
        small_send[step, 2 * PAD : 2 * PAD + SINKS, :] = sink_v[named] * live
        small_send[step, 3 * PAD : 3 * PAD + steps, :] = decode_v[named] * live
        for head in range(heads):
            columns = slice(head * HEAD_DIM, (head + 1) * HEAD_DIM)
            place = (4 + head) * PAD
            small_send[step, place : place + steps, :] = decode_q[named, :, columns] * live
        small_meta[step, 0:8, :] = jnp.full((8, 128), history[named] * active, jnp.int32)
        small_meta[step, 8:16, :] = jnp.full((8, 128), lengths[named] * active, jnp.int32)
        return carry

    lax.fori_loop(0, ring, prepare_queries, 0)

    @pl.when(z == y)
    def _():
        lax.fori_loop(0, ring, prepare_small, 0)

    pl.semaphore_wait(barrier, 2 * (ring - 1))

    def z_copy(number, place, size, step):
        rows = pl.ds(place, size)
        return pltpu.make_async_remote_copy(
            send.at[step, rows],
            stage.at[step, rows],
            z_send.at[number, step],
            z_recv.at[number, step],
            device_id=(around(z, step), tensor, y),
            device_id_type=MESH,
        )

    def y_copy(number, place, size, step, source, target):
        rows = pl.ds(place, size)
        return pltpu.make_async_remote_copy(
            stage.at[step, rows],
            final.at[source, rows],
            y_send.at[number, step],
            y_recv.at[number, source],
            device_id=(z, tensor, target),
            device_id_type=MESH,
        )

    def own_copy(number, place, size, step):
        rows = pl.ds(place, size)
        return pltpu.make_async_copy(
            stage.at[step, rows], final.at[y, rows], own_sem.at[number]
        )

    def query_part(number):
        return number, pl.multiple_of(number * query_size, 16), query_size

    def key_part(number):
        place = pl.multiple_of(head_rows + number * key_size, 16)
        return number + QUERY_STAGES, place, key_size

    steps_out = sorted(range(1, ring), key=lambda step: -min(step, ring - step))
    steps_in = [0] + steps_out[::-1]

    def spread(part):
        for step in steps_out:
            z_copy(*part, step).start()

    def forward(part):
        for step in steps_in:
            home = around(z, -step)
            if step:
                z_copy(*part, step).wait_recv()

            @pl.when(home != y)
            def _():
                y_copy(*part, step, y, home).start()

            @pl.when(home == y)
            def _():
                own_copy(*part, step).start()

    def arrive(part):
        own_copy(*part, 0).wait()
        for step in range(1, ring):
            source = around(y, step)
            y_copy(*part, 0, source, source).wait_recv()

    def small_copies(step):
        target = (around(z, step), tensor, y)
        return (
            pltpu.make_async_remote_copy(
                small_send.at[step],
                small,
                small_send_sem.at[0, step],
                small_recv_sem.at[0],
                device_id=target,
                device_id_type=MESH,
            ),
            pltpu.make_async_remote_copy(
                small_meta.at[step],
                meta,
                small_send_sem.at[1, step],
                small_recv_sem.at[1],
                device_id=target,
                device_id_type=MESH,
            ),
        )

    def small_own():
        return (
            pltpu.make_async_copy(small_send.at[0], small, small_own_sem.at[0]),
            pltpu.make_async_copy(small_meta.at[0], meta, small_own_sem.at[1]),
        )

    for number in range(AHEAD):
        spread(query_part(number))

    lax.fori_loop(0, ring, prepare_window, 0)

    @pl.when(z == y)
    def _():
        for step in steps_out:
            for copy in small_copies(step):
                copy.start()
        for copy in small_own():
            copy.start()

    def early(number, carry):
        spread(query_part(number + AHEAD))
        forward(query_part(number))
        return carry

    def late(number, carry):
        spread(key_part(number + AHEAD - QUERY_STAGES))
        forward(query_part(number))
        return carry

    lax.fori_loop(0, QUERY_STAGES - AHEAD, early, 0)
    lax.fori_loop(QUERY_STAGES - AHEAD, QUERY_STAGES, late, 0)

    def arrive_queries(number, carry):
        arrive(query_part(number))
        return carry

    for number in range(2):
        spread(key_part(number + AHEAD))
        forward(key_part(number))
    lax.fori_loop(0, QUERY_STAGES, arrive_queries, 0)

    @pl.when(z == y)
    def _():
        for copy in small_own():
            copy.wait()

    @pl.when(z != y)
    def _():
        for copy in small_copies(1):
            copy.wait_recv()

    def block_of(place, size):
        return final[:, pl.ds(place, size), :].reshape(ring * size, HEAD_DIM)

    def queries_of(head):
        extra = small[(4 + head) * PAD : (5 + head) * PAD, :]
        return jnp.concatenate([block_of(head * turn_rows, turn_rows), extra], axis=0)

    def scores_of(queries, keys):
        return lax.dot_general(
            queries,
            keys,
            (((1,), (1,)), ((), ())),
            preferred_element_type=jnp.float32,
        )

    def with_ones(values):
        return jnp.concatenate([values, jnp.ones_like(values)], axis=1)

    prior = meta[0:1, 0:1]
    length = meta[8:9, 0:1]

    def row_numbers(shape):
        return lax.broadcasted_iota(jnp.int32, shape, 0)

    def column_numbers(shape):
        return lax.broadcasted_iota(jnp.int32, shape, 1)

    first = (query_rows, turn + 2 * PAD)
    row, column = row_numbers(first), column_numbers(first)
    in_turn = row < turn
    limit = jnp.where(in_turn, row, length - 1)
    number = column - turn - PAD
    sees = (
        ((column < turn) & (column <= limit))
        | ((column >= turn) & (column < turn + SINKS))
        | ((number >= 0) & (number < steps) & (number <= row - turn))
    )
    bias[...] = jnp.where(sees, 0.0, NEG)
    first_keys = jnp.concatenate(
        [block_of(heads * turn_rows, turn_rows), small[0 : 2 * PAD, :]], axis=0
    )
    first_values = with_ones(
        jnp.concatenate(
            [block_of((heads + 1) * turn_rows, turn_rows), small[2 * PAD : 4 * PAD, :]], axis=0
        )
    )

    def start_head(head):
        scores = scores_of(queries_of(head), first_keys) + bias[...]
        top = jnp.max(scores, axis=1, keepdims=True)
        weights = jnp.exp2((scores - top) * scale).astype(jnp.bfloat16)
        peak[head] = jnp.broadcast_to(top, (query_rows, HEAD_DIM))
        total[head] = jnp.dot(weights, first_values, preferred_element_type=jnp.float32)

    for head in range(heads):
        start_head(head)

    def out_copies(number):
        place = pl.multiple_of(head_rows + number * key_size, 16)
        rows = pl.ds(pl.multiple_of(number * chunk, 16), chunk)
        return (
            pltpu.make_async_copy(
                final.at[:, pl.ds(place, chunk)], keys_out.at[:, rows], out_sem.at[0, number]
            ),
            pltpu.make_async_copy(
                final.at[:, pl.ds(place + chunk, chunk)],
                values_out.at[:, rows],
                out_sem.at[1, number],
            ),
        )

    def consume(number):
        arrive(key_part(number))
        for copy in out_copies(number):
            copy.start()
        place = pl.multiple_of(head_rows + number * key_size, 16)
        values = with_ones(block_of(place + chunk, chunk))
        shape = (width, HEAD_DIM)
        row, column = row_numbers(shape), column_numbers(shape)
        position = lax.div(row, chunk) * window_rows + number * chunk + lax.rem(row, chunk)
        gone = (column == 0) & (position < window + SINKS - prior)
        marked = (column == row + 1) & (row < chunk)
        marks = jnp.where(gone, NEG, jnp.where(marked, 1.0, 0.0)).astype(jnp.bfloat16)
        keys = jnp.concatenate([block_of(place, chunk), marks], axis=1)
        shape = (query_rows, HEAD_DIM)
        row, column = row_numbers(shape), column_numbers(shape)
        limit = jnp.where(row < turn, row, length + row - turn)
        passed = (column >= 1) & (number * chunk + column - 1 <= limit)
        flags = jnp.where(column == 0, 1.0, jnp.where(passed, NEG, 0.0)).astype(jnp.bfloat16)

        def one_head(head):
            scores = scores_of(jnp.concatenate([queries_of(head), flags], axis=1), keys)
            before = peak[head]
            top = jnp.maximum(before, jnp.max(scores, axis=1, keepdims=True))
            spread_top = jnp.concatenate([top] * (width // HEAD_DIM), axis=1)
            weights = jnp.exp2((scores - spread_top) * scale).astype(jnp.bfloat16)
            factor = jnp.exp2((before - top) * scale)
            peak[head] = top
            total[head] = total[head] * jnp.concatenate([factor] * 2, axis=1) + jnp.dot(
                weights, values, preferred_element_type=jnp.float32
            )

        for head in range(heads):
            one_head(head)

    def round_trip(number, carry):
        @pl.when(number + AHEAD < stages)
        def _():
            spread(key_part(number + AHEAD))

        @pl.when(number < stages)
        def _():
            forward(key_part(number))

        consume(number - 2)
        return carry

    lax.fori_loop(2, stages + 2, round_trip, 0)

    shown = row_numbers((turn, HEAD_DIM)) < length
    for head in range(heads):
        columns = slice(head * HEAD_DIM, (head + 1) * HEAD_DIM)
        result = total[head, :, 0:HEAD_DIM] / total[head, :, HEAD_DIM : 2 * HEAD_DIM]
        turn_out[:, columns] = jnp.where(shown, result[0:turn], 0.0).astype(jnp.bfloat16)
        decode_out[:, columns] = result[turn : turn + steps].astype(jnp.bfloat16)

    def finish(part):
        for step in range(ring):
            if step:
                z_copy(*part, step).wait_send()
            home = around(z, -step)

            @pl.when(home != y)
            def _():
                y_copy(*part, step, y, home).wait_send()

    def finish_queries(number, carry):
        finish(query_part(number))
        return carry

    def finish_keys(number, carry):
        finish(key_part(number))
        for copy in out_copies(number):
            copy.wait()
        return carry

    lax.fori_loop(0, QUERY_STAGES, finish_queries, 0)
    lax.fori_loop(0, stages, finish_keys, 0)

    @pl.when(z == y)
    def _():
        for step in steps_out:
            for copy in small_copies(step):
                copy.wait_send()


def shards(
    cache_keys,
    cache_values,
    sink_keys,
    sink_values,
    turn_queries,
    turn_keys,
    turn_values,
    decode_queries,
    decode_keys,
    decode_values,
    turn_lengths,
    history,
    targets,
):
    ring = lax.axis_size("ctx")
    window_rows = cache_keys.shape[1]
    turn_rows = turn_keys.shape[1]
    columns = turn_queries.shape[2]
    heads = columns // HEAD_DIM
    steps = decode_queries.shape[1]
    stages = 8
    query_rows = ring * turn_rows + PAD
    rows = (heads + 2) * turn_rows + 2 * window_rows
    small_rows = (4 + heads) * PAD
    count = QUERY_STAGES + stages
    vmem = pl.BlockSpec(memory_space=pltpu.VMEM)
    smem = pl.BlockSpec(memory_space=pltpu.SMEM)
    hbm = pl.BlockSpec(memory_space=pl.ANY)
    turn_out, decode_out, keys_out, values_out = pl.pallas_call(
        functools.partial(kernel, ring, stages),
        out_shape=(
            jax.ShapeDtypeStruct((ring * turn_rows, columns), jnp.bfloat16),
            jax.ShapeDtypeStruct((steps, columns), jnp.bfloat16),
            jax.ShapeDtypeStruct((ring, window_rows, HEAD_DIM), jnp.bfloat16),
            jax.ShapeDtypeStruct((ring, window_rows, HEAD_DIM), jnp.bfloat16),
        ),
        in_specs=[smem] * 3 + [vmem] * 10,
        out_specs=(vmem, vmem, hbm, hbm),
        scratch_shapes=[
            pltpu.VMEM((ring, rows, HEAD_DIM), jnp.bfloat16),
            pltpu.VMEM((ring, rows, HEAD_DIM), jnp.bfloat16),
            pltpu.VMEM((ring, rows, HEAD_DIM), jnp.bfloat16),
            pltpu.VMEM((ring, small_rows, HEAD_DIM), jnp.bfloat16),
            pltpu.VMEM((ring, 16, HEAD_DIM), jnp.int32),
            pltpu.VMEM((small_rows, HEAD_DIM), jnp.bfloat16),
            pltpu.VMEM((16, HEAD_DIM), jnp.int32),
            pltpu.VMEM((heads, query_rows, HEAD_DIM), jnp.float32),
            pltpu.VMEM((heads, query_rows, 2 * HEAD_DIM), jnp.float32),
            pltpu.VMEM((query_rows, ring * turn_rows + 2 * PAD), jnp.float32),
            pltpu.SemaphoreType.DMA((count, ring)),
            pltpu.SemaphoreType.DMA((count, ring)),
            pltpu.SemaphoreType.DMA((count, ring)),
            pltpu.SemaphoreType.DMA((count, ring)),
            pltpu.SemaphoreType.DMA((count,)),
            pltpu.SemaphoreType.DMA((2, ring)),
            pltpu.SemaphoreType.DMA((2,)),
            pltpu.SemaphoreType.DMA((2,)),
            pltpu.SemaphoreType.DMA((2, stages)),
        ],
        compiler_params=pltpu.CompilerParams(
            collective_id=0, has_side_effects=True, vmem_limit_bytes=56 * 1024 * 1024
        ),
    )(
        turn_lengths,
        history,
        targets[:, 0],
        cache_keys,
        cache_values,
        sink_keys,
        sink_values,
        turn_queries,
        turn_keys,
        turn_values,
        decode_queries,
        decode_keys,
        decode_values,
    )
    return (
        turn_out[None],
        decode_out[None],
        keys_out.reshape(1, ring * window_rows, HEAD_DIM),
        values_out.reshape(1, ring * window_rows, HEAD_DIM),
    )


def solution(mesh):
    whole = P("group", "ctx", "tensor")
    front = P("group", None, "tensor")
    slots = P(("group", "ctx"), None, "tensor")
    return jax.shard_map(
        shards,
        mesh=mesh,
        in_specs=(
            whole,
            whole,
            front,
            front,
            whole,
            whole,
            whole,
            front,
            front,
            front,
            P("group"),
            P("group"),
            P("group", None),
        ),
        out_specs=(slots,) * 4,
        check_vma=False,
    )
```

time: 341 us -> 125 us (0.37)
  the two profiles are of different devices: /device:TPU:2 before, /device:TPU:16 now
where the time goes in v1:
time: 125 us
  Pallas kernels  120 us (96%)
  local copies, waits for them, and re-layouts  4.99 us (4%)
    pallas_call x1, Pallas kernels, shards(): pl.pallas_call(functools.partial(kernel, ring, stages), out_shape=(jax.Sh...  120 us
    unnamed x10, local copies, waits for them, and re-layouts  4.99 us

profile of v1, /device:TPU:16, one launch (start us, length us, event | category | flops | bytes accessed | tf_op | source)
XLA Modules:
  0.0 125.3 jit_solution(1467633220218666961)
XLA Ops:
  0.6 119.6 %shard_map.156 = (bf16[384,1536]{1,0:T(8,128)(2,1)}, bf16[2,1536]{1,0:T(2,128)(2,1)}, bf16[8,512,128]{2,1,0:T(8,128)(2,1)}, bf16[8,512,128]{2,1,0:T(8,128)(2,1)}) custom-call(s32[4]{0:T(128)} %lengths.1, s32[4]{0:T(128)} %history.1, s32[4]{0:T(128)} %bitcast.9, bf16[4,512,128]{2,1,0:T(8,128)(2,1)} %cache_k.1, bf16[4,512,128]{2,1,0:T(8,128)(2,1)} %cache_v.1, ...), custom_call_target="tpu_custom_call" | custom-call | tf_op jit(solution)/shard_map/pallas_call | solution.py:470
  120.3 0.0 copy-start.2
  120.3 0.0 copy-start.1
  120.3 2.4 %copy.21 = bf16[1,384,1536]{2,1,0:T(8,128)(2,1)} copy(bf16[1,384,1536]{2,1,0:T(8,128)(2,1)} %bitcast.5) | data formatting | bytes 2359296
  122.7 0.0 copy-done.2
  122.7 0.0 copy-start
  122.7 0.6 copy.22
  123.3 0.0 copy-done.1
  123.3 1.0 copy.23
  124.3 0.0 copy-done
  124.3 1.0 copy.24
Async XLA Ops:
  120.3 2.5 %copy-start.2 = (bf16[2,1536]{1,0:T(2,128)(2,1)S(1)}, bf16[2,1536]{1,0:T(2,128)(2,1)}, u32[]{:S(2)}) copy-start(bf16[2,1536]{1,0:T(2,128)(2,1)} %get-tuple-element.9) | copy-start | bytes 18436
  120.3 3.1 %copy-start.1 = (bf16[8,512,128]{2,1,0:T(8,128)(2,1)S(1)}, bf16[8,512,128]{2,1,0:T(8,128)(2,1)}, u32[]{:S(2)}) copy-start(bf16[8,512,128]{2,1,0:T(8,128)(2,1)} %get-tuple-element.10) | copy-start | bytes 3145732
  122.7 1.6 %copy-start = (bf16[8,512,128]{2,1,0:T(8,128)(2,1)S(1)}, bf16[8,512,128]{2,1,0:T(8,128)(2,1)}, u32[]{:S(2)}) copy-start(bf16[8,512,128]{2,1,0:T(8,128)(2,1)} %get-tuple-element.11) | copy-start | bytes 3145732

commit v2 on v1

--- a/solution.py
+++ b/solution.py
@@ -13,16 +13,33 @@
 NEG = -1e30
 MESH = pl.DeviceIdType.MESH
 PAD = 16
-QUERY_STAGES = 6
+BLOCKS = 8
 AHEAD = 3
+BEHIND = 2
 
 
 def kernel(
     ring,
-    stages,
     lengths,
     history,
     targets,
+    cache_k_in,
+    cache_v_in,
+    sink_k_in,
+    sink_v_in,
+    turn_q_in,
+    turn_k_in,
+    turn_v_in,
+    decode_q_in,
+    decode_k_in,
+    decode_v_in,
+    turn_out,
+    decode_out,
+    keys_out,
+    values_out,
+    send,
+    stage,
+    final,
     cache_k,
     cache_v,
     sink_k,
@@ -33,17 +50,12 @@
     decode_q,
     decode_k,
     decode_v,
-    turn_out,
-    decode_out,
-    keys_out,
-    values_out,
-    send,
-    stage,
-    final,
+    in_sem,
     small_send,
     small_meta,
     small,
     meta,
+    extra,
     peak,
     total,
     bias,
@@ -68,14 +80,34 @@
     turn = turn_rows * ring
     query_rows = turn + PAD
     head_rows = (heads + 2) * turn_rows
-    query_size = head_rows // QUERY_STAGES
-    chunk = window_rows // stages
-    key_size = 2 * chunk
-    width = ring * chunk
+    chunk = window_rows // BLOCKS
+    whole = BLOCKS - 1
+    query_stages = (heads + 2 - 2) // 2 + 2
+    cuts = [(number * chunk, chunk) for number in range(whole)]
+    cuts += [(whole * chunk + half * chunk // 2, chunk // 2) for half in range(2)]
     scale = math.log2(math.e) / math.sqrt(HEAD_DIM)
 
     def around(place, step):
         return lax.rem(place + step + ring, ring)
+
+    def load(number, source, place):
+        return pltpu.make_async_copy(source, place, in_sem.at[number])
+
+    query_loads = (
+        load(0, turn_q_in, turn_q),
+        load(1, turn_k_in, turn_k),
+        load(2, turn_v_in, turn_v),
+    )
+    window_loads = (load(3, cache_k_in, cache_k), load(4, cache_v_in, cache_v))
+    small_loads = (
+        load(5, sink_k_in, sink_k),
+        load(6, sink_v_in, sink_v),
+        load(7, decode_q_in, decode_q),
+        load(8, decode_k_in, decode_k),
+        load(9, decode_v_in, decode_v),
+    )
+    for copy in query_loads + small_loads + window_loads:
+        copy.start()
 
     barrier = pltpu.get_barrier_semaphore()
     for step in range(1, ring):
@@ -95,34 +127,35 @@
             active = jnp.maximum(active, hit)
         return named, active
 
-    def put(step, place, size, value):
-        @pl.when(step == 0)
-        def _():
-            stage[0, pl.ds(place, size), :] = value
-
-        @pl.when(step != 0)
-        def _():
-            send[step, pl.ds(place, size), :] = value
-
-    def prepare_queries(step, carry):
+    def prepare_queries(step, place):
         named, active = chosen(around(z, step))
         live = active.astype(jnp.float32).astype(jnp.bfloat16)
         for head in range(heads):
             columns = slice(head * HEAD_DIM, (head + 1) * HEAD_DIM)
-            put(step, head * turn_rows, turn_rows, turn_q[named, :, columns] * live)
-        put(step, heads * turn_rows, turn_rows, turn_k[named] * live)
-        put(step, (heads + 1) * turn_rows, turn_rows, turn_v[named] * live)
-        return carry
-
-    def prepare_window(step, carry):
+            rows = slice(head * turn_rows, (head + 1) * turn_rows)
+            place[step, rows, :] = turn_q[named, :, columns] * live
+        rows = slice(heads * turn_rows, (heads + 1) * turn_rows)
+        place[step, rows, :] = turn_k[named] * live
+        rows = slice((heads + 1) * turn_rows, (heads + 2) * turn_rows)
+        place[step, rows, :] = turn_v[named] * live
+
+    def prepare_window(step, place):
         named, active = chosen(around(z, step))
         live = active.astype(jnp.float32).astype(jnp.bfloat16)
-        for number in range(stages):
-            rows = slice(number * chunk, (number + 1) * chunk)
-            place = head_rows + number * key_size
-            put(step, place, chunk, cache_k[named, rows, :] * live)
-            put(step, place + chunk, chunk, cache_v[named, rows, :] * live)
-        return carry
+        for start, size in cuts:
+            rows = slice(start, start + size)
+            first = head_rows + 2 * start
+            place[step, first : first + size, :] = cache_k[named, rows, :] * live
+            place[step, first + size : first + 2 * size, :] = cache_v[named, rows, :] * live
+
+    def prepare(part):
+        part(0, stage)
+
+        def one_step(step, carry):
+            part(step, send)
+            return carry
+
+        lax.fori_loop(1, ring, one_step, 0)
 
     def prepare_small(step, carry):
         named, active = chosen(around(z, step))
@@ -134,17 +167,15 @@
         small_send[step, 3 * PAD : 3 * PAD + steps, :] = decode_v[named] * live
         for head in range(heads):
             columns = slice(head * HEAD_DIM, (head + 1) * HEAD_DIM)
-            place = (4 + head) * PAD
-            small_send[step, place : place + steps, :] = decode_q[named, :, columns] * live
-        small_meta[step, 0:8, :] = jnp.full((8, 128), history[named] * active, jnp.int32)
-        small_meta[step, 8:16, :] = jnp.full((8, 128), lengths[named] * active, jnp.int32)
+            start = 4 * PAD + head * steps
+            small_send[step, start : start + steps, :] = decode_q[named, :, columns] * live
+        first_row = lax.broadcasted_iota(jnp.int32, small_meta.shape[1:], 0) == 0
+        small_meta[step] = jnp.where(first_row, history[named], lengths[named]) * active
         return carry
 
-    lax.fori_loop(0, ring, prepare_queries, 0)
-
-    @pl.when(z == y)
-    def _():
-        lax.fori_loop(0, ring, prepare_small, 0)
+    for copy in query_loads:
+        copy.wait()
+    prepare(prepare_queries)
 
     pl.semaphore_wait(barrier, 2 * (ring - 1))
 
@@ -176,12 +207,18 @@
             stage.at[step, rows], final.at[y, rows], own_sem.at[number]
         )
 
+    def short_part(number):
+        return number, number * turn_rows, turn_rows
+
     def query_part(number):
-        return number, pl.multiple_of(number * query_size, 16), query_size
+        return number, pl.multiple_of((number - 1) * 2 * turn_rows, 16), 2 * turn_rows
 
     def key_part(number):
-        place = pl.multiple_of(head_rows + number * key_size, 16)
-        return number + QUERY_STAGES, place, key_size
+        place = pl.multiple_of(head_rows + number * 2 * chunk, 16)
+        return number + query_stages, place, 2 * chunk
+
+    def end_part(half):
+        return query_stages + whole + half, head_rows + 2 * cuts[whole + half][0], chunk
 
     steps_out = sorted(range(1, ring), key=lambda step: -min(step, ring - step))
     steps_in = [0] + steps_out[::-1]
@@ -209,6 +246,16 @@
         for step in range(1, ring):
             source = around(y, step)
             y_copy(*part, 0, source, source).wait_recv()
+
+    def finish(part):
+        for step in range(ring):
+            if step:
+                z_copy(*part, step).wait_send()
+            home = around(z, -step)
+
+            @pl.when(home != y)
+            def _():
+                y_copy(*part, step, y, home).wait_send()
 
     def small_copies(step):
         target = (around(z, step), tensor, y)
@@ -237,13 +284,18 @@
             pltpu.make_async_copy(small_meta.at[0], meta, small_own_sem.at[1]),
         )
 
-    for number in range(AHEAD):
-        spread(query_part(number))
-
-    lax.fori_loop(0, ring, prepare_window, 0)
+    for part in (short_part(0), short_part(1), query_part(2)):
+        spread(part)
+
+    for copy in window_loads:
+        copy.wait()
+    prepare(prepare_window)
+    for copy in small_loads:
+        copy.wait()
 
     @pl.when(z == y)
     def _():
+        lax.fori_loop(0, ring, prepare_small, 0)
         for step in steps_out:
             for copy in small_copies(step):
                 copy.start()
@@ -256,21 +308,28 @@
         return carry
 
     def late(number, carry):
-        spread(key_part(number + AHEAD - QUERY_STAGES))
+        spread(key_part(number + AHEAD - query_stages))
         forward(query_part(number))
         return carry
 
-    lax.fori_loop(0, QUERY_STAGES - AHEAD, early, 0)
-    lax.fori_loop(QUERY_STAGES - AHEAD, QUERY_STAGES, late, 0)
-
-    def arrive_queries(number, carry):
-        arrive(query_part(number))
-        return carry
-
     for number in range(2):
+        spread(query_part(number + AHEAD))
+        forward(short_part(number))
+    lax.fori_loop(2, query_stages - AHEAD, early, 0)
+    lax.fori_loop(query_stages - AHEAD, query_stages, late, 0)
+    for number in range(BEHIND):
         spread(key_part(number + AHEAD))
         forward(key_part(number))
-    lax.fori_loop(0, QUERY_STAGES, arrive_queries, 0)
+
+    def settle_queries(number, carry):
+        arrive(query_part(number))
+        finish(query_part(number))
+        return carry
+
+    for number in range(2):
+        arrive(short_part(number))
+        finish(short_part(number))
+    lax.fori_loop(2, query_stages, settle_queries, 0)
 
     @pl.when(z == y)
     def _():
@@ -286,8 +345,7 @@
         return final[:, pl.ds(place, size), :].reshape(ring * size, HEAD_DIM)
 
     def queries_of(head):
-        extra = small[(4 + head) * PAD : (5 + head) * PAD, :]
-        return jnp.concatenate([block_of(head * turn_rows, turn_rows), extra], axis=0)
+        return jnp.concatenate([block_of(head * turn_rows, turn_rows), extra[head]], axis=0)
 
     def scores_of(queries, keys):
         return lax.dot_general(
@@ -301,7 +359,7 @@
         return jnp.concatenate([values, jnp.ones_like(values)], axis=1)
 
     prior = meta[0:1, 0:1]
-    length = meta[8:9, 0:1]
+    length = meta[1:2, 0:1]
 
     def row_numbers(shape):
         return lax.broadcasted_iota(jnp.int32, shape, 0)
@@ -320,6 +378,15 @@
         | ((number >= 0) & (number < steps) & (number <= row - turn))
     )
     bias[...] = jnp.where(sees, 0.0, NEG)
+    packed = small[4 * PAD :, :]
+    shape = (PAD, packed.shape[0])
+    row, column = row_numbers(shape), column_numbers(shape)
+    for head in range(heads):
+        picks = (row < steps) & (column == head * steps + row)
+        picks = jnp.where(picks, 1.0, 0.0).astype(jnp.bfloat16)
+        extra[head] = jnp.dot(picks, packed, preferred_element_type=jnp.float32).astype(
+            jnp.bfloat16
+        )
     first_keys = jnp.concatenate(
         [block_of(heads * turn_rows, turn_rows), small[0 : 2 * PAD, :]], axis=0
     )
@@ -339,37 +406,42 @@
     for head in range(heads):
         start_head(head)
 
-    def out_copies(number):
-        place = pl.multiple_of(head_rows + number * key_size, 16)
-        rows = pl.ds(pl.multiple_of(number * chunk, 16), chunk)
+    shown = row_numbers((turn, HEAD_DIM)) < length
+
+    def out_copies(start, size, number):
+        place = head_rows + 2 * start
+        rows = pl.ds(pl.multiple_of(start, 16), size)
         return (
             pltpu.make_async_copy(
-                final.at[:, pl.ds(place, chunk)], keys_out.at[:, rows], out_sem.at[0, number]
+                final.at[:, pl.ds(pl.multiple_of(place, 16), size)],
+                keys_out.at[:, rows],
+                out_sem.at[0, number],
             ),
             pltpu.make_async_copy(
-                final.at[:, pl.ds(place + chunk, chunk)],
+                final.at[:, pl.ds(pl.multiple_of(place + size, 16), size)],
                 values_out.at[:, rows],
                 out_sem.at[1, number],
             ),
         )
 
-    def consume(number):
-        arrive(key_part(number))
-        for copy in out_copies(number):
+    def consume(part, start, size, number, last):
+        arrive(part)
+        for copy in out_copies(start, size, number):
             copy.start()
-        place = pl.multiple_of(head_rows + number * key_size, 16)
-        values = with_ones(block_of(place + chunk, chunk))
+        width = ring * size
+        place = pl.multiple_of(head_rows + 2 * start, 16)
+        values = with_ones(block_of(pl.multiple_of(place + size, 16), size))
         shape = (width, HEAD_DIM)
         row, column = row_numbers(shape), column_numbers(shape)
-        position = lax.div(row, chunk) * window_rows + number * chunk + lax.rem(row, chunk)
+        position = lax.div(row, size) * window_rows + start + lax.rem(row, size)
         gone = (column == 0) & (position < window + SINKS - prior)
-        marked = (column == row + 1) & (row < chunk)
+        marked = (column == row + 1) & (row < size)
         marks = jnp.where(gone, NEG, jnp.where(marked, 1.0, 0.0)).astype(jnp.bfloat16)
-        keys = jnp.concatenate([block_of(place, chunk), marks], axis=1)
+        keys = jnp.concatenate([block_of(place, size), marks], axis=1)
         shape = (query_rows, HEAD_DIM)
         row, column = row_numbers(shape), column_numbers(shape)
         limit = jnp.where(row < turn, row, length + row - turn)
-        passed = (column >= 1) & (number * chunk + column - 1 <= limit)
+        passed = (column >= 1) & (start + column - 1 <= limit)
         flags = jnp.where(column == 0, 1.0, jnp.where(passed, NEG, 0.0)).astype(jnp.bfloat16)
 
         def one_head(head):
@@ -379,57 +451,61 @@
             spread_top = jnp.concatenate([top] * (width // HEAD_DIM), axis=1)
             weights = jnp.exp2((scores - spread_top) * scale).astype(jnp.bfloat16)
             factor = jnp.exp2((before - top) * scale)
-            peak[head] = top
-            total[head] = total[head] * jnp.concatenate([factor] * 2, axis=1) + jnp.dot(
+            sums = total[head] * jnp.concatenate([factor] * 2, axis=1) + jnp.dot(
                 weights, values, preferred_element_type=jnp.float32
             )
+            if not last:
+                peak[head] = top
+                total[head] = sums
+                return
+            columns = slice(head * HEAD_DIM, (head + 1) * HEAD_DIM)
+            result = sums[:, 0:HEAD_DIM] / sums[:, HEAD_DIM : 2 * HEAD_DIM]
+            turn_out[:, columns] = jnp.where(shown, result[0:turn], 0.0).astype(jnp.bfloat16)
+            decode_out[:, columns] = result[turn : turn + steps].astype(jnp.bfloat16)
 
         for head in range(heads):
             one_head(head)
 
     def round_trip(number, carry):
-        @pl.when(number + AHEAD < stages)
+        @pl.when(number + AHEAD < whole)
         def _():
             spread(key_part(number + AHEAD))
 
-        @pl.when(number < stages)
+        @pl.when(number < whole)
         def _():
             forward(key_part(number))
 
-        consume(number - 2)
+        for half in range(2):
+
+            @pl.when(number + AHEAD == whole + half)
+            def _():
+                spread(end_part(half))
+
+            @pl.when(number == whole + half)
+            def _():
+                forward(end_part(half))
+
+        done = number - BEHIND
+        consume(key_part(done), done * chunk, chunk, done, False)
+        finish(key_part(done))
         return carry
 
-    lax.fori_loop(2, stages + 2, round_trip, 0)
-
-    shown = row_numbers((turn, HEAD_DIM)) < length
-    for head in range(heads):
-        columns = slice(head * HEAD_DIM, (head + 1) * HEAD_DIM)
-        result = total[head, :, 0:HEAD_DIM] / total[head, :, HEAD_DIM : 2 * HEAD_DIM]
-        turn_out[:, columns] = jnp.where(shown, result[0:turn], 0.0).astype(jnp.bfloat16)
-        decode_out[:, columns] = result[turn : turn + steps].astype(jnp.bfloat16)
-
-    def finish(part):
-        for step in range(ring):
-            if step:
-                z_copy(*part, step).wait_send()
-            home = around(z, -step)
-
-            @pl.when(home != y)
-            def _():
-                y_copy(*part, step, y, home).wait_send()
-
-    def finish_queries(number, carry):
-        finish(query_part(number))
-        return carry
-
-    def finish_keys(number, carry):
-        finish(key_part(number))
-        for copy in out_copies(number):
+    lax.fori_loop(BEHIND, whole + BEHIND, round_trip, 0)
+    for half in range(2):
+        consume(end_part(half), *cuts[whole + half], whole + half, half == 1)
+
+    finish(end_part(0))
+    finish(end_part(1))
+
+    def finish_copies(number, carry):
+        for copy in out_copies(number * chunk, chunk, number):
             copy.wait()
         return carry
 
-    lax.fori_loop(0, QUERY_STAGES, finish_queries, 0)
-    lax.fori_loop(0, stages, finish_keys, 0)
+    lax.fori_loop(0, whole, finish_copies, 0)
+    for half in range(2):
+        for copy in out_copies(*cuts[whole + half], whole + half):
+            copy.wait()
 
     @pl.when(z == y)
     def _():
@@ -459,32 +535,47 @@
     columns = turn_queries.shape[2]
     heads = columns // HEAD_DIM
     steps = decode_queries.shape[1]
-    stages = 8
     query_rows = ring * turn_rows + PAD
     rows = (heads + 2) * turn_rows + 2 * window_rows
-    small_rows = (4 + heads) * PAD
-    count = QUERY_STAGES + stages
+    small_rows = 4 * PAD + -(-heads * steps // PAD) * PAD
+    count = heads // 2 + 2 + BLOCKS + 1
+    arrays = (
+        cache_keys,
+        cache_values,
+        sink_keys,
+        sink_values,
+        turn_queries,
+        turn_keys,
+        turn_values,
+        decode_queries,
+        decode_keys,
+        decode_values,
+    )
     vmem = pl.BlockSpec(memory_space=pltpu.VMEM)
     smem = pl.BlockSpec(memory_space=pltpu.SMEM)
-    hbm = pl.BlockSpec(memory_space=pl.ANY)
+    hbm = pl.BlockSpec(memory_space=pltpu.HBM)
+    free = pl.BlockSpec(memory_space=pl.ANY)
     turn_out, decode_out, keys_out, values_out = pl.pallas_call(
-        functools.partial(kernel, ring, stages),
+        functools.partial(kernel, ring),
         out_shape=(
             jax.ShapeDtypeStruct((ring * turn_rows, columns), jnp.bfloat16),
             jax.ShapeDtypeStruct((steps, columns), jnp.bfloat16),
             jax.ShapeDtypeStruct((ring, window_rows, HEAD_DIM), jnp.bfloat16),
             jax.ShapeDtypeStruct((ring, window_rows, HEAD_DIM), jnp.bfloat16),
         ),
-        in_specs=[smem] * 3 + [vmem] * 10,
-        out_specs=(vmem, vmem, hbm, hbm),
+        in_specs=[smem] * 3 + [hbm] * 10,
+        out_specs=(vmem, vmem, free, free),
         scratch_shapes=[
             pltpu.VMEM((ring, rows, HEAD_DIM), jnp.bfloat16),
             pltpu.VMEM((ring, rows, HEAD_DIM), jnp.bfloat16),
             pltpu.VMEM((ring, rows, HEAD_DIM), jnp.bfloat16),
+            *[pltpu.VMEM(a.shape, a.dtype) for a in arrays],
+            pltpu.SemaphoreType.DMA((len(arrays),)),
             pltpu.VMEM((ring, small_rows, HEAD_DIM), jnp.bfloat16),
-            pltpu.VMEM((ring, 16, HEAD_DIM), jnp.int32),
+            pltpu.VMEM((ring, 8, HEAD_DIM), jnp.int32),
             pltpu.VMEM((small_rows, HEAD_DIM), jnp.bfloat16),
-            pltpu.VMEM((16, HEAD_DIM), jnp.int32),
+            pltpu.VMEM((8, HEAD_DIM), jnp.int32),
+            pltpu.VMEM((heads, PAD, HEAD_DIM), jnp.bfloat16),
             pltpu.VMEM((heads, query_rows, HEAD_DIM), jnp.float32),
             pltpu.VMEM((heads, query_rows, 2 * HEAD_DIM), jnp.float32),
             pltpu.VMEM((query_rows, ring * turn_rows + 2 * PAD), jnp.float32),
@@ -496,7 +587,7 @@
             pltpu.SemaphoreType.DMA((2, ring)),
             pltpu.SemaphoreType.DMA((2,)),
             pltpu.SemaphoreType.DMA((2,)),
-            pltpu.SemaphoreType.DMA((2, stages)),
+            pltpu.SemaphoreType.DMA((2, BLOCKS + 1)),
         ],
         compiler_params=pltpu.CompilerParams(
             collective_id=0, has_side_effects=True, vmem_limit_bytes=56 * 1024 * 1024
@@ -505,16 +596,7 @@
         turn_lengths,
         history,
         targets[:, 0],
-        cache_keys,
-        cache_values,
-        sink_keys,
-        sink_values,
-        turn_queries,
-        turn_keys,
-        turn_values,
-        decode_queries,
-        decode_keys,
-        decode_values,
+        *arrays,
     )
     return (
         turn_out[None],

time: 125 us -> 116 us (0.928)
  the two profiles are of different devices: /device:TPU:16 before, /device:TPU:58 now
where the time goes in v2:
time: 116 us
  Pallas kernels  111 us (96%)
  local copies, waits for them, and re-layouts  4.99 us (4%)
    pallas_call x1, Pallas kernels, shards(): pl.pallas_call(functools.partial(kernel, ring), out_shape=(jax.ShapeDtype...  111 us
    unnamed x10, local copies, waits for them, and re-layouts  4.99 us

profile of v2, /device:TPU:58, one launch (start us, length us, event | category | flops | bytes accessed | tf_op | source)
XLA Modules:
  0.0 116.3 jit_solution(15091548225527789265)
XLA Ops:
  0.6 110.6 %shard_map.156 = (bf16[384,1536]{1,0:T(8,128)(2,1)}, bf16[2,1536]{1,0:T(2,128)(2,1)}, bf16[8,512,128]{2,1,0:T(8,128)(2,1)}, bf16[8,512,128]{2,1,0:T(8,128)(2,1)}) custom-call(s32[4]{0:T(128)} %lengths.1, s32[4]{0:T(128)} %history.1, s32[4]{0:T(128)} %bitcast.9, bf16[4,512,128]{2,1,0:T(8,128)(2,1)} %cache_k_in.1, bf16[4,512,128]{2,1,0:T(8,128)(2,1)} %cache_v_in.1, ...), custom_call_target="tpu_custom_call" | custom-call | tf_op jit(solution)/shard_map/pallas_call | solution.py:558
  111.3 0.0 copy-start.2
  111.3 0.0 copy-start.1
  111.3 2.4 %copy.21 = bf16[1,384,1536]{2,1,0:T(8,128)(2,1)} copy(bf16[1,384,1536]{2,1,0:T(8,128)(2,1)} %bitcast.5) | data formatting | bytes 2359296
  113.7 0.0 copy-done.2
  113.7 0.0 copy-start
  113.7 0.6 copy.22
  114.3 0.0 copy-done.1
  114.3 1.0 copy.23
  115.3 0.0 copy-done
  115.3 1.0 copy.24
Async XLA Ops:
  111.3 2.5 %copy-start.2 = (bf16[2,1536]{1,0:T(2,128)(2,1)S(1)}, bf16[2,1536]{1,0:T(2,128)(2,1)}, u32[]{:S(2)}) copy-start(bf16[2,1536]{1,0:T(2,128)(2,1)} %get-tuple-element.9) | copy-start | bytes 18436
  111.3 3.1 %copy-start.1 = (bf16[8,512,128]{2,1,0:T(8,128)(2,1)S(1)}, bf16[8,512,128]{2,1,0:T(8,128)(2,1)}, u32[]{:S(2)}) copy-start(bf16[8,512,128]{2,1,0:T(8,128)(2,1)} %get-tuple-element.10) | copy-start | bytes 3145732
  113.7 1.6 %copy-start = (bf16[8,512,128]{2,1,0:T(8,128)(2,1)S(1)}, bf16[8,512,128]{2,1,0:T(8,128)(2,1)}, u32[]{:S(2)}) copy-start(bf16[8,512,128]{2,1,0:T(8,128)(2,1)} %get-tuple-element.11) | copy-start | bytes 3145732

commit v3 on v2

--- a/solution.py
+++ b/solution.py
@@ -514,6 +514,51 @@
                 copy.wait_send()
 
 
+PIECES = 4
+
+
+def settle(
+    turn_in,
+    decode_in,
+    keys_in,
+    values_in,
+    turn_out,
+    decode_out,
+    keys_out,
+    values_out,
+    turn_held,
+    keys_held,
+    values_held,
+    come,
+    gone,
+):
+    arriving, leaving = [], []
+    for number, (source, held, place) in enumerate(
+        (
+            (keys_in, keys_held, keys_out),
+            (values_in, values_held, values_out),
+            (turn_in, turn_held, turn_out),
+        )
+    ):
+        size = source.shape[0] // PIECES
+        for piece in range(PIECES):
+            rows = pl.ds(piece * size, size)
+            arriving.append(
+                pltpu.make_async_copy(source.at[rows], held.at[rows], come.at[number, piece])
+            )
+            leaving.append(
+                pltpu.make_async_copy(held.at[rows], place.at[rows], gone.at[number, piece])
+            )
+    for copy in arriving:
+        copy.start()
+    decode_out[...] = decode_in[...]
+    for before, after in zip(arriving, leaving):
+        before.wait()
+        after.start()
+    for copy in leaving:
+        copy.wait()
+
+
 def shards(
     cache_keys,
     cache_values,
@@ -555,7 +600,7 @@
     smem = pl.BlockSpec(memory_space=pltpu.SMEM)
     hbm = pl.BlockSpec(memory_space=pltpu.HBM)
     free = pl.BlockSpec(memory_space=pl.ANY)
-    turn_out, decode_out, keys_out, values_out = pl.pallas_call(
+    outs = pl.pallas_call(
         functools.partial(kernel, ring),
         out_shape=(
             jax.ShapeDtypeStruct((ring * turn_rows, columns), jnp.bfloat16),
@@ -598,6 +643,20 @@
         targets[:, 0],
         *arrays,
     )
+    turn_out, decode_out, keys_out, values_out = pl.pallas_call(
+        settle,
+        out_shape=tuple(jax.ShapeDtypeStruct(a.shape, a.dtype) for a in outs),
+        in_specs=[hbm, vmem, hbm, hbm],
+        out_specs=(hbm, vmem, hbm, hbm),
+        scratch_shapes=[
+            pltpu.VMEM(outs[0].shape, jnp.bfloat16),
+            pltpu.VMEM(outs[2].shape, jnp.bfloat16),
+            pltpu.VMEM(outs[3].shape, jnp.bfloat16),
+            pltpu.SemaphoreType.DMA((3, PIECES)),
+            pltpu.SemaphoreType.DMA((3, PIECES)),
+        ],
+        compiler_params=pltpu.CompilerParams(vmem_limit_bytes=56 * 1024 * 1024),
+    )(*outs)
     return (
         turn_out[None],
         decode_out[None],

time: 116 us -> 116 us (level)
  local copies, waits for them, and re-layouts: 4.99 us -> 0 us
  Pallas kernels: 111 us -> 115 us
    unnamed x10 -> x0, local copies, waits for them, and re-layouts: 4.99 us -> none
    pallas_call x0 -> x1, Pallas kernels: none -> 4.14 us  [shards(): pl.pallas_call(settle, out_shape=tuple((jax.ShapeDtypeStruct(a.shape, a.d...]
where the time goes in v3:
time: 116 us; the launch traced here: 115 us
  Pallas kernels  115 us (99%)
    pallas_call x1, Pallas kernels, shards(): pl.pallas_call(functools.partial(kernel, ring), out_shape=(jax.ShapeDtype...  111 us
    pallas_call x1, Pallas kernels, shards(): pl.pallas_call(settle, out_shape=tuple((jax.ShapeDtypeStruct(a.shape, a.d...  4.14 us

profile of v3, /device:TPU:58, one launch (start us, length us, event | category | flops | bytes accessed | tf_op | source)
XLA Modules:
  0.0 115.4 jit_solution(924779369503249678)
XLA Ops:
  0.6 110.6 %shard_map.156 = (bf16[384,1536]{1,0:T(8,128)(2,1)}, bf16[2,1536]{1,0:T(2,128)(2,1)}, bf16[8,512,128]{2,1,0:T(8,128)(2,1)}, bf16[8,512,128]{2,1,0:T(8,128)(2,1)}) custom-call(s32[4]{0:T(128)} %lengths.1, s32[4]{0:T(128)} %history.1, s32[4]{0:T(128)} %bitcast.5, bf16[4,512,128]{2,1,0:T(8,128)(2,1)} %cache_k_in.1, bf16[4,512,128]{2,1,0:T(8,128)(2,1)} %cache_v_in.1, ...), custom_call_target="tpu_custom_call" | custom-call | tf_op jit(solution)/shard_map/pallas_call | solution.py:603
  111.3 4.1 %shard_map.157 = (bf16[384,1536]{1,0:T(8,128)(2,1)}, bf16[2,1536]{1,0:T(2,128)(2,1)}, bf16[8,512,128]{2,1,0:T(8,128)(2,1)}, bf16[8,512,128]{2,1,0:T(8,128)(2,1)}) custom-call(bf16[384,1536]{1,0:T(8,128)(2,1)} %get-tuple-element.12.turn_in, bf16[2,1536]{1,0:T(2,128)(2,1)} %get-tuple-element.13.decode_in, bf16[8,512,128]{2,1,0:T(8,128)(2,1)} %get-tuple-element.14.keys_in, ...), custom_call_target="tpu_custom_call" | custom-call | tf_op jit(solution)/shard_map/pallas_call | solution.py:646
